TPU v7x, 32 devices: a whole 2x2x4 slice. The times are simulated.
32 devices in a mesh: work: 8 (over y, x, core), tile: 4 (over z).
Axes of the slice: x: 2, y: 2, z: 4, core: 2. Of those that a mesh axis runs over, the one named last changes fastest.
Arguments:
- block_coords: float32 [4096, 3, 128], P(('work', 'tile')), may hold values from -6 to 6
- block_visibilities: float32 [4096, 4, 128], P(('work', 'tile')), may hold values from -6 to 6
- subgrid_of_block: int32 [4096], P(('work', 'tile')), may hold values from 0 to 127, as said below
- live_blocks: int32 [32], P(('work', 'tile')), may hold values from 96 to 128, as said below
- corners: int32 [128, 2], replicated, may hold values from 0 to 992, as said below
- channel_scale: float32 [2], replicated, may hold values from 0.85 to 1.15
Outputs:
- uv_grid: float32 [4, 256, 1024], P(None, 'tile', 'work')
Inputs may be any that keep to these rules, and one draw needn't show every extreme that they name: `subgrid_of_block`: subgrid s belongs to the strip of worker s // 16. Among the 128 blocks of one device at most 64 belong to subgrids of one worker, and some worker gets exactly 64 blocks from every device. Device d in the order of the axes work, tile holds the blocks d * 128 to (d + 1) * 128 - 1; its first live_blocks[d] blocks are live, the others take no part. Some device has all its blocks live. Subgrid s covers rows corners[s, 0] to corners[s, 0] + 31 of the window, and columns corners[s, 1] to corners[s, 1] + 31, all inside columns 128 (s // 16) to 128 (s // 16 + 1) - 1.
All inputs are finite; a program needn't handle non-finite values.
Results may differ from a plain program's by a relative error of at most 0.0003.
Values sent between devices are 32-bit elements; how exact they have to be, the bound alone decides.
A program may use at most 192 MiB of HBM per device.

v0:
```python
import math

import jax
import jax.numpy as jnp
from jax import lax
from jax.sharding import PartitionSpec as P

CH = 2
SUB = 32
ROWS = 128
TR = 64
GCW = 128
SUBW = 16


two_pi = 2.0 * math.pi
highest = lax.Precision.HIGHEST


def pixel_offsets():
    return (jnp.arange(SUB, dtype=jnp.float32) - SUB // 2) / SUB


def block_pictures(coords, waves, channel_scale):
    offsets = pixel_offsets()
    squares = offsets * offsets
    layers = []
    for channel in range(CH):
        factor = channel_scale[channel]
        first_coord = coords[:, 0, :] * factor
        second_coord = coords[:, 1, :] * factor
        depth_coord = coords[:, 2, :] * factor
        depth_term = depth_coord[:, None, :] * squares[None, :, None]
        phase_first = two_pi * (first_coord[:, None, :] * offsets[None, :, None] + depth_term)
        phase_second = two_pi * (second_coord[:, None, :] * offsets[None, :, None] + depth_term)
        wave_real = waves[:, 2 * channel, :][:, None, :]
        wave_imag = waves[:, 2 * channel + 1, :][:, None, :]
        cosine_first = jnp.cos(phase_first)
        sine_first = jnp.sin(phase_first)
        cosine_second = jnp.cos(phase_second)
        sine_second = jnp.sin(phase_second)
        left_side = jnp.concatenate(
            [
                wave_real * cosine_first - wave_imag * sine_first,
                wave_real * sine_first + wave_imag * cosine_first,
            ],
            axis=2,
        )
        right_real = jnp.concatenate([cosine_second, -sine_second], axis=2)
        right_imag = jnp.concatenate([sine_second, cosine_second], axis=2)
        right_side = jnp.concatenate([right_real, right_imag], axis=1)
        layers.append(jnp.einsum("nxk,njk->nxj", left_side, right_side, precision=highest))
    return jnp.stack(layers, axis=1)


def transform_matrix():
    offsets = jnp.arange(SUB, dtype=jnp.int32)
    taper_values = jnp.sin(jnp.pi * (offsets.astype(jnp.float32) + 0.5) / SUB) ** 2
    product = offsets[:, None] * offsets[None, :] % SUB
    angles = two_pi * product.astype(jnp.float32) / SUB
    real_part = taper_values[:, None] * jnp.cos(angles)
    imag_part = -taper_values[:, None] * jnp.sin(angles)
    upper = jnp.concatenate([real_part, imag_part], axis=1)
    lower = jnp.concatenate([-imag_part, real_part], axis=1)
    return jnp.concatenate([upper, lower], axis=0)


def to_spectrum(pictures):
    amount = pictures.shape[0]
    matrix = transform_matrix()
    first = jnp.einsum("ncxj,jq->ncxq", pictures, matrix, precision=highest)
    first = first.reshape(amount, CH, SUB, 2, SUB)
    second = jnp.einsum(
        "ncxpl,pxqk->ncqkl", first, matrix.reshape(2, SUB, 2, SUB), precision=highest
    )
    return (second * (1.0 / (ROWS * SUB))).reshape(amount, 2 * CH, SUB, SUB)


def place_dense(spectra, row_start, col_start, height, width):
    offsets = jnp.arange(SUB, dtype=jnp.int32)
    row_cells = jnp.arange(height, dtype=jnp.int32)
    col_cells = jnp.arange(width, dtype=jnp.int32)
    row_map = (
        row_cells[None, :, None] == row_start[:, None, None] + offsets[None, None, :]
    ).astype(jnp.float32)
    col_map = (
        col_start[:, None, None] + offsets[None, :, None] == col_cells[None, None, :]
    ).astype(jnp.float32)
    widened = jnp.einsum("spkl,slj->spkj", spectra, col_map, precision=highest)
    return jnp.einsum("sik,spkj->pij", row_map, widened, precision=highest)


def merge_pictures(selector, pictures):
    slots = pictures.shape[0]
    merged = jnp.dot(selector, pictures.reshape(slots, CH * SUB * 2 * SUB), precision=highest)
    return merged.reshape(SUBW, CH, SUB, 2 * SUB)


def local(block_coords, block_visibilities, subgrid_of_block, live_blocks, corners, channel_scale):
    workers = lax.axis_size("work")
    tiles = lax.axis_size("tile")
    worker = lax.axis_index("work")
    blocks = block_coords.shape[0]
    capacity = 4 * blocks // workers
    position = jnp.arange(blocks, dtype=jnp.int32)
    owner = jnp.where(position < live_blocks[0], subgrid_of_block // SUBW, workers)
    earlier = (owner[:, None] == owner[None, :]) & (position[None, :] < position[:, None])
    before = jnp.sum(earlier.astype(jnp.int32), axis=1)
    target = owner * capacity + before
    payload = jnp.concatenate([block_coords, block_visibilities], axis=1)
    slot_ids = jnp.arange(workers * capacity, dtype=jnp.int32)
    matches = slot_ids[:, None] == target[None, :]
    dispatch = matches.astype(jnp.float32)
    send_data = jnp.dot(
        dispatch, payload.reshape(blocks, payload.shape[1] * payload.shape[2]), precision=highest
    )
    send_labels = jnp.sum(jnp.where(matches, subgrid_of_block[None, :] + 1, 0), axis=1) - 1
    send_data = send_data.reshape(workers, capacity, payload.shape[1], payload.shape[2])
    send_labels = send_labels.reshape(workers, capacity)
    payloads = lax.all_to_all(send_data, "work", split_axis=0, concat_axis=0, tiled=True)
    labels = lax.all_to_all(send_labels, "work", split_axis=0, concat_axis=0, tiled=True)
    leading = payloads.shape[0]
    items = payloads.shape[1]
    flat = payloads.reshape(leading * items, payloads.shape[2], payloads.shape[3])
    pictures = block_pictures(flat[:, 0:3, :], flat[:, 3:, :], channel_scale)
    pictures, got_labels = (pictures.reshape(leading, items, CH, SUB, 2 * SUB), labels)
    slots = pictures.shape[0] * pictures.shape[1]
    pictures = pictures.reshape(slots, CH, SUB, 2 * SUB)
    local_labels = got_labels.reshape(slots) - worker * SUBW
    local_corners = lax.dynamic_slice_in_dim(corners, worker * SUBW, SUBW, 0)
    col_corners = local_corners[:, 1] - worker * GCW
    subgrid_ids = jnp.arange(SUBW, dtype=jnp.int32)
    height = TR * tiles
    selector = (subgrid_ids[:, None] == local_labels[None, :]).astype(jnp.float32)
    merged = merge_pictures(selector, pictures)
    spectra = to_spectrum(merged)
    strip = place_dense(spectra, local_corners[:, 0], col_corners, height, GCW)
    uv_grid = lax.psum_scatter(strip, "tile", scatter_dimension=1, tiled=True)
    return uv_grid


def solution(mesh):
    return jax.shard_map(
        local,
        mesh=mesh,
        in_specs=(
            P(("work", "tile"), None, None),
            P(("work", "tile"), None, None),
            P(("work", "tile")),
            P(("work", "tile")),
            P(),
            P(),
        ),
        out_specs=P(None, "tile", "work"),
        check_vma=False,
    )
```

profile of v0, /device:TPU:0, one launch (start us, length us, event | category | flops | bytes accessed | tf_op | source)
XLA Modules:
  0.0 336.9 jit_solution(3645769925268223156)
XLA Ops:
  6.5 0.0 copy-start
  7.2 0.7 broadcast_add_fusion.1
  7.9 0.2 convert_reduce_fusion
  8.1 0.2 select_reduce_fusion
  8.2 0.7 sub.60
  8.9 5.2 %all-to-all-start = ((s32[8,1,64]{2,1,0:T(1,128)}), s32[8,1,64]{2,1,0:T(1,128)S(1)}, u32[]{:S(2)}, u32[]{:S(2)}) async-start(s32[8,1,64]{2,1,0:T(1,128)} %sub.60), calls=%async_computation | async-start | bytes 8192 | tf_op jit(solution)/shard_map/all_to_all | solution.py:121
  14.1 1.1 copy.32
  15.2 1.1 copy.31
  16.2 2.2 fusion.58
  18.4 0.3 all-to-all-done
  18.7 3.9 %all-to-all-start.1 = ((f32[8,64,7,128]{3,1,2,0:T(8,128)}), f32[8,64,7,128]{3,1,2,0:T(8,128)S(1)}, u32[]{:S(2)}, u32[]{:S(2)}) async-start(f32[8,64,7,128]{3,1,2,0:T(8,128)} %fusion.58), calls=%async_computation.1 | async-start | bytes 3670016 | tf_op jit(solution)/shard_map/all_to_all | solution.py:120
  22.6 0.0 all-reduce.3.cloned.1.call-start
  22.7 0.1 cosine_multiply_fusion
  22.8 0.1 sine_multiply_fusion
  22.9 0.1 maximum_maximum_fusion
  23.0 0.1 reshape.140
  23.1 0.0 copy-done
  23.1 0.1 constant_dynamic-slice_fusion.1
  23.2 1.4 fusion.87
  24.6 0.1 iota_add_fusion
  24.7 0.1 sub.63
  24.8 21.7 %all-to-all-done.1 = f32[8,64,7,128]{3,1,2,0:T(8,128)S(1)} async-done(((f32[8,64,7,128]{3,1,2,0:T(8,128)}), f32[8,64,7,128]{3,1,2,0:T(8,128)S(1)}, u32[]{:S(2)}, u32[]{:S(2)}) %all-to-all-start.1) | async-done | bytes 1835040 | tf_op jit(solution)/shard_map/all_to_all | solution.py:120
  46.4 0.2 copy.33
  46.6 1.5 slice_bitcast_fusion.3
  48.2 133.9 %multiply_subtract_fusion.1 = (f32[512,32,128]{2,1,0:T(8,128)}, f32[512,32,128]{2,1,0:T(8,128)}, f32[512,32,128]{2,1,0:T(8,128)}, f32[512,32,128]{2,1,0:T(8,128)...) fusion(f32[512,128]{1,0:T(8,128)S(1)} %get-tuple-element.12, ...), kind=kLoop, calls=%fused_computation.42 | loop fusion | flops 58720256 | bytes 86507776 | tf_op jit(solution)/shard_map/sub | solution.py:44
  182.1 35.4 %fusion.41 = f32[512,1,32,64]{3,2,0,1:T(8,128)} fusion(f32[512,32,128]{2,1,0:T(8,128)} %get-tuple-element.26, f32[512,32,128]{2,1,0:T(8,128)} %get-tuple-element.25, f32[512,32,128]{2,1,0:T(8,128)} %get-tuple-element.27, f32[512,32,128]{2,1,0:T(8,128)} %get-tuple-element.16, f32[512,32,128]{2,1,0:T(8,128)} %get-tuple-element.15), kind=kOutput, calls=%fused_computation.46 | convolution fusion | flops 3250585600 | bytes 46137344 | tf_op jit(solution)/shard_map/nxk,njk->nxj/dot_general | solution.py:52
  217.5 35.8 %fusion.36 = f32[512,1,32,64]{3,2,0,1:T(8,128)} fusion(f32[512,32,128]{2,1,0:T(8,128)} %get-tuple-element.34, f32[512,32,128]{2,1,0:T(8,128)} %get-tuple-element.35, f32[512,32,128]{2,1,0:T(8,128)} %get-tuple-element.33, f32[512,32,128]{2,1,0:T(8,128)} %get-tuple-element.36, f32[512,32,128]{2,1,0:T(8,128)} %get-tuple-element.37), kind=kOutput, calls=%fused_computation.45 | convolution fusion | flops 3250585600 | bytes 46137344 | tf_op jit(solution)/shard_map/nxk,njk->nxj/dot_general | solution.py:52
  253.3 11.8 %pad_maximum_fusion = f32[512,2,32,64]{3,2,0,1:T(8,128)} fusion(f32[512,1,32,64]{3,2,0,1:T(8,128)} %fusion.36, f32[512,1,32,64]{3,2,0,1:T(8,128)} %fusion.41), kind=kLoop, calls=%fused_computation.22 | loop fusion | flops 2097152 | bytes 16777216 | tf_op jit(solution)/shard_map/stack | solution.py:53
  265.1 12.8 %copy.34 = f32[512,2,32,64]{0,3,2,1:T(8,128)} copy(f32[512,2,32,64]{3,2,0,1:T(8,128)} %pad_maximum_fusion) | data formatting | bytes 16777216 | tf_op jit(solution)/shard_map/stack | solution.py:53
  277.8 0.0 copy-start.2
  277.9 0.0 copy-start.1
  277.9 7.5 %fusion.26 = f32[16,2,32,64]{3,0,2,1:T(8,128)S(1)} fusion(f32[512,2,32,64]{0,3,2,1:T(8,128)} %copy.34, s32[512]{0:T(512)S(1)} %sub.63), kind=kOutput, calls=%fused_computation.31 | convolution fusion | flops 402661376 | bytes 8652800 | tf_op jit(solution)/shard_map/dot_general | solution.py:95
  285.4 0.7 fusion.54
  286.1 0.6 reshape.143
  286.7 1.1 fusion.49
  287.7 0.1 copy.38
  287.8 0.7 fusion.51
  288.5 1.1 convolution_bitcast_fusion.1
  289.6 1.0 copy.40
  290.6 0.0 all-reduce.3.cloned.1.call-update
  290.6 0.0 copy-done.2
  290.7 0.6 dynamic-slice
  291.9 36.6 %all-reduce.3.cloned.1.call-done = f32[4,256,128]{2,0,1:T(4,128)} async-done(((f32[4,256,128]{2,0,1:T(4,128)}), f32[4,256,128]{2,0,1:T(4,128)}) %all-reduce.3.cloned.1.call-update) | async-done | bytes 524304
  328.5 0.9 constant_dynamic-slice_fusion
  329.4 0.7 copy.41
  330.1 0.0 copy-done.1
  (8 shorter events, 0.1 us)
Async XLA Ops:
  6.5 16.6 %copy-start = (s32[128,2]{0,1:T(2,128)S(1)}, s32[128,2]{0,1:T(2,128)}, u32[]{:S(2)}) copy-start(s32[128,2]{0,1:T(2,128)} %param.10) | copy-start | bytes 3076
  8.9 9.8 %all-to-all-start = ((s32[8,1,64]{2,1,0:T(1,128)}), s32[8,1,64]{2,1,0:T(1,128)S(1)}, u32[]{:S(2)}, u32[]{:S(2)}) async-start(s32[8,1,64]{2,1,0:T(1,128)} %sub.60), calls=%async_computation | async-start | bytes 8192 | tf_op jit(solution)/shard_map/all_to_all | solution.py:121
  18.7 27.8 %all-to-all-start.1 = ((f32[8,64,7,128]{3,1,2,0:T(8,128)}), f32[8,64,7,128]{3,1,2,0:T(8,128)S(1)}, u32[]{:S(2)}, u32[]{:S(2)}) async-start(f32[8,64,7,128]{3,1,2,0:T(8,128)} %fusion.58), calls=%async_computation.1 | async-start | bytes 3670016 | tf_op jit(solution)/shard_map/all_to_all | solution.py:120
  22.6 305.9 %all-reduce.3.cloned.1.call-start = ((), (), s32[]{:S(2)}) async-start(), calls=%async_computation.2 | async-start | bytes 1048576
  277.8 12.8 %copy-start.2 = (u32[32]{0:T(128)S(1)}, u32[32]{0:T(128)}, u32[]{:S(2)}) copy-start(u32[32]{0:T(128)} %constant.73) | copy-start | bytes 388
  277.9 52.2 %copy-start.1 = (s32[128,2]{0,1:T(2,128)S(1)}, s32[128,2]{0,1:T(2,128)}, u32[]{:S(2)}) copy-start(s32[128,2]{0,1:T(2,128)} %param.10) | copy-start | bytes 3076
Sparse Core Ops, SparseCore 0:
  290.8 37.6 all-reduce.2
where the time goes:
time: 337 us
  other arithmetic  149 us (44%)
  matrix products  84.4 us (25%)
  waiting for transfers between devices  58.5 us (17%)
  local copies, waits for them, and re-layouts  21.3 us (6%)
  between operations  14.9 us (4%)
  starting transfers between devices  9.14 us (3%)
    sub x1, other arithmetic, block_pictures(): wave_real * cosine_first - wave_imag * sine_first  134 us
    dot_general x2, matrix products, block_pictures(): jnp.einsum('nxk,njk->nxj', left_side, right_side, precision=highest)  71.2 us
    unnamed x2, waiting for transfers between devices  36.6 us
    all_to_all x1, waiting for transfers between devices, local(): lax.all_to_all(send_data, 'work', split_axis=0, concat_axis=0, tiled=True)  21.7 us
    another operation x1, local copies, waits for them, and re-layouts, block_pictures(): return jnp.stack(layers, axis=1)  12.8 us
    another operation x1, other arithmetic, block_pictures(): return jnp.stack(layers, axis=1)  11.8 us
    dot_general x1, matrix products, merge_pictures(): jnp.dot(selector, pictures.reshape(slots, CH * SUB * 2 * SUB), precision=...  7.52 us
  transfers between devices with their start and end apart: 3, of which 3 were waited for; matrix products, arithmetic and copies ran while one was open for 2% of the time, Pallas kernels for 0%

commit v1 on v0

v1 whole, which is shorter than its diff:
```python
import functools
import math

import jax
import jax.numpy as jnp
import numpy as np
from jax import lax
from jax.experimental import pallas as pl
from jax.experimental.pallas import tpu as pltpu
from jax.sharding import PartitionSpec as P

CH = 2
SUB = 32
ROWS = 128
GCW = 128
SUBW = 16
HALF = SUBW // 2
UNROLL = 4
MESH = pl.DeviceIdType.MESH
highest = lax.Precision.HIGHEST

SIN = (6.283184916495431, -41.34158923268848, 81.59994332978006, -76.61447253122435, 41.34288235446963, -12.471243534886277)
COS = (0.9999992107823215, -19.73898035576396, 64.92865742103214, -85.2716215342875, 58.7904921200778, -21.07110562755528)


def horner(coefficients, z):
    total = jnp.full_like(z, coefficients[-1])
    for value in coefficients[-2::-1]:
        total = total * z + value
    return total


def sincos_turns(turns):
    rest = turns - jnp.round(turns)
    z = rest * rest
    return rest * horner(SIN, z), horner(COS, z)


def split(value):
    high = value.astype(jnp.bfloat16)
    return high, (value - high.astype(jnp.float32)).astype(jnp.bfloat16)


def dot_nt(left, right):
    return lax.dot_general(left, right, (((1,), (1,)), ((), ())), preferred_element_type=jnp.float32)


def pictures_kernel(labels_ref, live_ref, scale_ref, coords_ref, waves_ref, out_ref):
    blocks = coords_ref.shape[0]
    out_ref[...] = jnp.zeros_like(out_ref)
    offset = (lax.broadcasted_iota(jnp.int32, (SUB, ROWS), 0) - SUB // 2).astype(jnp.float32) * (1.0 / SUB)
    square = offset * offset
    low_lanes = lax.broadcasted_iota(jnp.int32, (SUB, 2 * CH * SUB), 1) < 2 * SUB
    live = live_ref[0]

    def picture(block):
        coords = coords_ref[block]
        waves = waves_ref[block] * (block < live).astype(jnp.float32)
        depth = coords[2:3, :] * square
        turns_first = coords[0:1, :] * offset + depth
        turns_second = coords[1:2, :] * offset + depth
        products = []
        for channel in range(CH):
            factor = scale_ref[channel]
            sine, cosine = sincos_turns(turns_first * factor)
            real, imag = waves[2 * channel:2 * channel + 1, :], waves[2 * channel + 1:2 * channel + 2, :]
            left_high, left_low = split(
                jnp.concatenate([real * cosine - imag * sine, real * sine + imag * cosine], axis=1)
            )
            sine, cosine = sincos_turns(turns_second * factor)
            sine_high, sine_low = split(sine)
            cosine_high, cosine_low = split(cosine)
            parts = [
                jnp.concatenate([cosine_high, -sine_high], axis=1),
                jnp.concatenate([sine_high, cosine_high], axis=1),
                jnp.concatenate([cosine_low, -sine_low], axis=1),
                jnp.concatenate([sine_low, cosine_low], axis=1),
            ]
            if channel == 1:
                parts = parts[2:] + parts[:2]
            product = dot_nt(jnp.concatenate([left_high, left_low], axis=0), jnp.concatenate(parts, axis=0))
            products.append(product[:SUB] + product[SUB:])
        first, second = products
        return jnp.where(low_lanes, first, second) + pltpu.roll(jnp.where(low_lanes, second, first), 2 * SUB, 1)

    def body(step, carry):
        base = step * UNROLL
        group = [picture(base + k) for k in range(UNROLL)]
        for k in range(UNROLL):
            label = labels_ref[base + k]
            out_ref[label] = out_ref[label] + group[k]
        return carry

    lax.fori_loop(0, blocks // UNROLL, body, 0)


def partial_pictures(coords, waves, labels, live, scale, subgrids):
    smem = pl.BlockSpec(memory_space=pltpu.SMEM)
    vmem = pl.BlockSpec(memory_space=pltpu.VMEM)
    return pl.pallas_call(
        pictures_kernel,
        out_shape=jax.ShapeDtypeStruct((subgrids, SUB, 2 * CH * SUB), jnp.float32),
        in_specs=[smem, smem, smem, vmem, vmem],
        out_specs=vmem,
        compiler_params=pltpu.CompilerParams(vmem_limit_bytes=32 * 1024 * 1024),
        name="block_pictures",
    )(labels, live, scale, coords, waves)


def transform_matrices():
    at = np.arange(SUB)
    taper = np.sin(np.pi * (at + 0.5) / SUB) ** 2
    angles = 2.0 * math.pi * (at[:, None] * at[None, :] % SUB) / SUB
    real, imag = taper[:, None] * np.cos(angles), -taper[:, None] * np.sin(angles)
    plain = np.block([[real, imag], [-imag, real]])
    turned = np.block([[-imag, real], [-real, -imag]])
    columns = np.concatenate([np.kron(np.eye(CH), plain), np.kron(np.eye(CH), turned)], axis=1)
    rows = np.concatenate([real.T, imag.T], axis=1) / (ROWS * SUB)
    return columns.astype(np.float32), rows.astype(np.float32)


def stage_shapes(workers):
    bits = workers.bit_length() - 1
    return [[0] * bits, [0] + [bits - 1 - step for step in range(1, bits)]]


def combine_kernel(workers, tiles, *refs):
    corners_ref, data_ref, columns_ref, rows_ref, out_ref = refs[:5]
    bits = workers.bit_length() - 1
    orders = stage_shapes(workers)
    scratch = list(refs[5:])
    received = [[scratch.pop(0) for _ in range(bits)] for _ in range(2)]
    kept = [[scratch.pop(0) for _ in range(bits)] for _ in range(2)]
    placed, outgoing, incoming, send_sem, recv_sem, tile_send, tile_recv = scratch
    worker, tile = lax.axis_index("work"), lax.axis_index("tile")
    height = out_ref.shape[1]

    def partner(bit):
        return worker + (1 << bit) * (1 - 2 * ((worker >> bit) & 1))

    barrier = pltpu.get_barrier_semaphore()
    for bit in range(bits):
        pl.semaphore_signal(barrier, inc=1, device_id=(partner(bit), tile), device_id_type=MESH)
    for far in range(1, tiles):
        pl.semaphore_signal(barrier, inc=1, device_id=(worker, lax.rem(tile + far, tiles)), device_id_type=MESH)
    pl.semaphore_wait(barrier, bits + tiles - 1)

    def step_copy(half, step):
        position = orders[half][step]
        bit = 0 if step == 0 else (step if half == 0 else bits - step)
        mine = (worker >> bit) & 1
        if step == 0:
            source = data_ref.at[:, 1 - mine, :, pl.ds(half * HALF, HALF)]
        else:
            source = kept[half][step - 1].at[:, 1 - mine]
        return mine, pltpu.make_async_remote_copy(
            src_ref=source,
            dst_ref=received[half][step],
            send_sem=send_sem.at[half, step],
            recv_sem=recv_sem.at[half, step],
            device_id=(partner(bit), tile),
            device_id_type=MESH,
        )

    def step_sum(half, step, mine):
        arrived = received[half][step]
        high, low = arrived.shape[:2]
        following = kept[half][step].shape
        for a in range(high):
            for b in range(low):
                at = a * low + b
                if step == 0:
                    own = data_ref[a, mine, b, pl.ds(half * HALF, HALF)]
                else:
                    own = kept[half][step - 1][a, mine, b]
                low_next = following[2]
                kept[half][step][at // (2 * low_next), at // low_next % 2, at % low_next] = own + arrived[a, b]

    def last_sum(half, mine):
        step = bits - 1
        own = data_ref[0, mine, 0, pl.ds(half * HALF, HALF)] if step == 0 else kept[half][step - 1][0, mine, 0]
        kept[half][step][...] = own + received[half][step][0, 0]

    copies = [step_copy(half, 0) for half in range(2)]
    for _, copy in copies:
        copy.start()
    for step in range(bits):
        for half in range(2):
            mine, copy = copies[half]
            copy.wait()
            if step < bits - 1:
                step_sum(half, step, mine)
                copies[half] = step_copy(half, step + 1)
                copies[half][1].start()
            else:
                last_sum(half, mine)

    width = 2 * CH * SUB
    columns, rows = columns_ref[...], rows_ref[...]
    lane = lax.broadcasted_iota(jnp.int32, (1, SUBW * SUB), 1)
    row_at = jnp.zeros((1, SUBW * SUB), jnp.int32)
    stripe = lax.broadcasted_iota(jnp.int32, (width, GCW), 0)
    across = lax.broadcasted_iota(jnp.int32, (width, GCW), 1) - stripe % SUB
    group = lax.broadcasted_iota(jnp.int32, (width, width), 0) // SUB
    same = group == lax.broadcasted_iota(jnp.int32, (width, width), 1) // SUB
    for half in range(2):
        pictures = kept[half][bits - 1][...].reshape(HALF * SUB, width)
        first = jnp.dot(pictures, columns, precision=highest, preferred_element_type=jnp.float32)
        for s in range(HALF):
            sub = half * HALF + s
            piece = first[s * SUB:(s + 1) * SUB]
            stacked = jnp.concatenate([piece[:, :width], piece[:, width:]], axis=0)
            spectrum = jnp.dot(rows, stacked, precision=highest, preferred_element_type=jnp.float32)
            spread = jnp.where(same, jnp.concatenate([spectrum] * (2 * CH), axis=0), 0.0)
            high, low = split(spread)
            row0 = corners_ref[worker * SUBW + sub, 0]
            col0 = corners_ref[worker * SUBW + sub, 1] - worker * GCW
            target = jnp.where(across == col0, 1.0, 0.0).astype(jnp.bfloat16)
            wide = jnp.dot(jnp.concatenate([high, low], axis=0), target, preferred_element_type=jnp.float32)
            wide = wide[:width] + wide[width:]
            high, low = split(wide)
            for p in range(2 * CH):
                placed[p, sub * SUB:(sub + 1) * SUB, :GCW] = high[p * SUB:(p + 1) * SUB]
                placed[p, sub * SUB:(sub + 1) * SUB, GCW:] = low[p * SUB:(p + 1) * SUB]
            row_at = jnp.where(lane // SUB == sub, row0 + lane % SUB, row_at)

    def tile_rows(which, store):
        line = lax.broadcasted_iota(jnp.int32, (height, SUBW * SUB), 0) + which * height
        select = jnp.where(line == row_at, 1.0, 0.0).astype(jnp.bfloat16)
        for p in range(2 * CH):
            both = jnp.dot(select, placed[p], preferred_element_type=jnp.float32)
            store[p] = both[:, :GCW] + both[:, GCW:]

    sent = []
    for far in range(tiles - 1, 0, -1):
        which = lax.rem(tile + far, tiles)
        tile_rows(which, outgoing.at[far - 1])
        copy = pltpu.make_async_remote_copy(
            src_ref=outgoing.at[far - 1],
            dst_ref=incoming.at[far - 1],
            send_sem=tile_send.at[far - 1],
            recv_sem=tile_recv.at[far - 1],
            device_id=(worker, which),
            device_id_type=MESH,
        )
        copy.start()
        sent.append(copy)
    tile_rows(tile, out_ref)
    for copy in sent:
        copy.wait()
    total = out_ref[...]
    for far in range(tiles - 1):
        total = total + incoming[far]
    out_ref[...] = total


def combine(pictures, corners, workers, tiles, height):
    bits = workers.bit_length() - 1
    received, kept = [], []
    for order in stage_shapes(workers):
        for step in range(bits):
            count = workers >> step
            low = 1 << order[step]
            tail = (HALF, SUB, 2 * CH * SUB)
            received.append(pltpu.VMEM((count // (2 * low), low) + tail, jnp.float32))
            if step < bits - 1:
                low = 1 << order[step + 1]
                kept.append(pltpu.VMEM((count // 2 // (2 * low), 2, low) + tail, jnp.float32))
            else:
                kept.append(pltpu.VMEM(tail, jnp.float32))
    columns, rows = transform_matrices()
    block = (2 * CH, height, GCW)
    vmem = pl.BlockSpec(memory_space=pltpu.VMEM)
    return pl.pallas_call(
        functools.partial(combine_kernel, workers, tiles),
        out_shape=jax.ShapeDtypeStruct(block, jnp.float32),
        in_specs=[pl.BlockSpec(memory_space=pltpu.SMEM), vmem, vmem, vmem],
        out_specs=vmem,
        scratch_shapes=received + kept + [
            pltpu.VMEM((2 * CH, SUBW * SUB, 2 * GCW), jnp.bfloat16),
            pltpu.VMEM((tiles - 1,) + block, jnp.float32),
            pltpu.VMEM((tiles - 1,) + block, jnp.float32),
            pltpu.SemaphoreType.DMA((2, bits)),
            pltpu.SemaphoreType.DMA((2, bits)),
            pltpu.SemaphoreType.DMA((tiles - 1,)),
            pltpu.SemaphoreType.DMA((tiles - 1,)),
        ],
        compiler_params=pltpu.CompilerParams(
            collective_id=0, has_side_effects=True, vmem_limit_bytes=48 * 1024 * 1024
        ),
        name="reduce_and_place",
    )(corners, pictures.reshape(workers // 2, 2, 1, SUBW, SUB, 2 * CH * SUB), jnp.asarray(columns), jnp.asarray(rows))


def local(height, block_coords, block_visibilities, subgrid_of_block, live_blocks, corners, channel_scale):
    workers = lax.axis_size("work")
    tiles = lax.axis_size("tile")
    pictures = partial_pictures(
        block_coords, block_visibilities, subgrid_of_block, live_blocks, channel_scale, corners.shape[0]
    )
    return combine(pictures, corners, workers, tiles, height)


def solution(mesh):
    height = 64
    return jax.shard_map(
        functools.partial(local, height),
        mesh=mesh,
        in_specs=(
            P(("work", "tile"), None, None),
            P(("work", "tile"), None, None),
            P(("work", "tile")),
            P(("work", "tile")),
            P(),
            P(),
        ),
        out_specs=P(None, "tile", "work"),
        check_vma=False,
    )
```

time: 337 us -> 60.7 us (0.18)
  other arithmetic: 149 us -> 0 us
  matrix products: 84.4 us -> 0 us
  waiting for transfers between devices: 58.5 us -> 0 us
  Pallas kernels: 0 us -> 55.7 us
  local copies, waits for them, and re-layouts: 21.3 us -> 4.15 us
  between operations: 14.9 us -> 0.69 us
  starting transfers between devices: 9.14 us -> 0 us
    sub x3 -> x0, other arithmetic: 134 us -> none  [the longest x1 134 us: block_pictures(): wave_real * cosine_first - wave_imag * sine_first]
    dot_general x8 -> x0, matrix products: 84.4 us -> none  [the longest x2 71.2 us: block_pictures(): jnp.einsum('nxk,njk->nxj', left_side, right_side, precision=highest)]
    pallas_call x0 -> x2, Pallas kernels: none -> 55.7 us  [the longest x1 38.3 us: combine(): pl.pallas_call(functools.partial(combine_kernel, workers, tiles), out_sha...]
    unnamed x2 -> x0, waiting for transfers between devices: 36.6 us -> none
    all_to_all x2 -> x0, waiting for transfers between devices: 21.9 us -> none  [the longest x1 21.7 us: local(): lax.all_to_all(send_data, 'work', split_axis=0, concat_axis=0, tiled=True)]
    another operation x1 -> x0, local copies, waits for them, and re-layouts: 12.8 us -> none  [block_pictures(): return jnp.stack(layers, axis=1)]
    another operation x1 -> x0, other arithmetic: 11.8 us -> none  [block_pictures(): return jnp.stack(layers, axis=1)]
    all_to_all x2 -> x0, starting transfers between devices: 9.1 us -> none  [the longest x1 5.17 us: local(): lax.all_to_all(send_labels, 'work', split_axis=0, concat_axis=0, tiled=True)]
  transfers between devices with their start and end apart: 3 -> 0, of which waited for: 3 -> 0; matrix products, arithmetic and copies ran while one was open for 2% -> 0% of each run, Pallas kernels for 0% -> 0%
where the time goes in v1:
time: 60.7 us; the launch traced here: 60.5 us
  Pallas kernels  55.7 us (92%)
  local copies, waits for them, and re-layouts  4.15 us (7%)
  between operations  0.69 us (1%)
    pallas_call x1, Pallas kernels, combine(): pl.pallas_call(functools.partial(combine_kernel, workers, tiles), out_sha...  38.3 us
    pallas_call x1, Pallas kernels, partial_pictures(): pl.pallas_call(pictures_kernel, out_shape=jax.ShapeDtypeStruct((subgrids,...  17.4 us
    unnamed x15, local copies, waits for them, and re-layouts  4.15 us

profile of v1, /device:TPU:0, one launch (start us, length us, event | category | flops | bytes accessed | tf_op | source)
XLA Modules:
  0.0 60.5 jit_solution(10756989536197961608)
XLA Ops:
  0.0 0.0 copy-start.1
  0.0 0.0 copy-start.2
  0.0 0.0 copy-start.5
  0.0 1.1 %copy.9.coords_ref = f32[128,3,128]{2,1,0:T(4,128)S(1)} copy(f32[128,3,128]{2,0,1:T(8,128)} %param.8) | data formatting | bytes 393216 | tf_op args[0]
  1.8 0.0 copy-start
  1.8 0.9 %copy-done = f32[128,4,128]{2,1,0:T(4,128)S(1)} copy-done((f32[128,4,128]{2,1,0:T(4,128)S(1)}, f32[128,4,128]{2,1,0:T(4,128)}, u32[]{:S(2)}) %copy-start) | copy-done | bytes 262168
  2.7 0.0 copy-start.3
  2.7 0.7 %copy-done.3 = s32[128]{0:T(128)S(1)} copy-done((s32[128]{0:T(128)S(1)}, s32[128]{0:T(128)}, u32[]{:S(2)}) %copy-start.3) | copy-done | bytes 536
  3.4 0.0 copy-start.4
  3.4 0.7 %copy-done.4 = f32[2]{0:T(128)S(1)} copy-done((f32[2]{0:T(128)S(1)}, f32[2]{0:T(128)}, u32[]{:S(2)}) %copy-start.4) | copy-done | bytes 32
  4.0 17.4 %block_pictures.1 = f32[128,32,128]{2,1,0:T(8,128)S(1)} custom-call(s32[128]{0:T(128)S(1)} %copy-done.3, s32[1]{0:T(128)S(6)} %copy.12.live_ref, f32[2]{0:T(128)S(1)} %copy-done.4, f32[128,3,128]{2,1,0:T(4,128)S(1)} %copy.9.coords_ref, f32[128,4,128]{2,1,0:T(4,128)S(1)} %copy-done), custom_call_target="tpu_custom_call" | custom-call | tf_op jit(solution)/shard_map/block_pictures/pallas_call | solution.py:100
  21.4 0.0 copy-done.5
  21.4 0.1 copy.10.refs_0_
  21.5 0.0 copy-done.1
  21.6 0.0 copy-done.2
  21.6 38.3 %reduce_and_place.1 = f32[4,64,128]{2,1,0:T(8,128)S(1)} custom-call(s32[128,2]{1,0:T(8,128)S(1)} %copy.10.refs_0_, f32[4,2,1,16,32,128]{5,4,3,2,1,0:T(8,128)S(1)} %bitcast.1, f32[128,256]{1,0:T(8,128)S(1)} %copy-done.1, f32[32,64]{1,0:T(8,128)S(1)} %copy-done.2), custom_call_target="tpu_custom_call" | custom-call | tf_op jit(solution)/shard_map/reduce_and_place/pallas_call | solution.py:274
  59.9 0.7 %copy.13 = f32[4,64,128]{2,1,0:T(8,128)} copy(f32[4,64,128]{2,1,0:T(8,128)S(1)} %reduce_and_place.1) | data formatting | bytes 262144
Async XLA Ops:
  0.0 21.5 %copy-start.1 = (f32[128,256]{1,0:T(8,128)S(1)}, f32[128,256]{1,0:T(8,128)}, u32[]{:S(2)}) copy-start(f32[128,256]{1,0:T(8,128)} %constant.4.clone.refs_2_) | copy-start | bytes 393220
  0.0 21.6 %copy-start.2 = (f32[32,64]{1,0:T(8,128)S(1)}, f32[32,64]{1,0:T(8,128)}, u32[]{:S(2)}) copy-start(f32[32,64]{1,0:T(8,128)} %constant.5.clone.refs_3_) | copy-start | bytes 24580
  0.0 21.4 %copy-start.5 = (s32[128,2]{0,1:T(2,128)S(1)}, s32[128,2]{0,1:T(2,128)}, u32[]{:S(2)}) copy-start(s32[128,2]{0,1:T(2,128)} %param.12) | copy-start | bytes 3076
  1.8 1.0 %copy-start = (f32[128,4,128]{2,1,0:T(4,128)S(1)}, f32[128,4,128]{2,1,0:T(4,128)}, u32[]{:S(2)}) copy-start(f32[128,4,128]{2,1,0:T(4,128)} %waves_ref.1) | copy-start | bytes 786436
  2.7 0.7 %copy-start.3 = (s32[128]{0:T(128)S(1)}, s32[128]{0:T(128)}, u32[]{:S(2)}) copy-start(s32[128]{0:T(128)} %labels_ref.1) | copy-start | bytes 1540
  3.4 0.7 %copy-start.4 = (f32[2]{0:T(128)S(1)}, f32[2]{0:T(128)}, u32[]{:S(2)}) copy-start(f32[2]{0:T(128)} %scale_ref.1) | copy-start | bytes 28

commit v2 on v1

v2 whole, which is shorter than its diff:
```python
import functools
import math

import jax
import jax.numpy as jnp
import numpy as np
from jax import lax
from jax.experimental import pallas as pl
from jax.experimental.pallas import tpu as pltpu
from jax.sharding import PartitionSpec as P

CH = 2
SUB = 32
ROWS = 128
GCW = 128
SUBW = 16
QUARTER = SUBW // 4
UNROLL = 4
MESH = pl.DeviceIdType.MESH
highest = lax.Precision.HIGHEST

SIN = (6.283184916495431, -41.34158923268848, 81.59994332978006, -76.61447253122435, 41.34288235446963, -12.471243534886277)
COS = (0.9999992107823215, -19.73898035576396, 64.92865742103214, -85.2716215342875, 58.7904921200778, -21.07110562755528)


def horner(coefficients, z):
    total = jnp.full_like(z, coefficients[-1])
    for value in coefficients[-2::-1]:
        total = total * z + value
    return total


def sincos_turns(turns):
    rest = turns - jnp.round(turns)
    z = rest * rest
    return rest * horner(SIN, z), horner(COS, z)


def split(value):
    high = value.astype(jnp.bfloat16)
    return high, (value - high.astype(jnp.float32)).astype(jnp.bfloat16)


def dot_nt(left, right):
    return lax.dot_general(left, right, (((1,), (1,)), ((), ())), preferred_element_type=jnp.float32)


def pictures_kernel(labels_hbm, live_ref, scale_ref, coords_hbm, waves_hbm, out_ref, labels_ref, coords_ref, waves_ref, sems):
    loads = [
        pltpu.make_async_copy(source, target, sems.at[at])
        for at, (source, target) in enumerate(
            [(labels_hbm, labels_ref), (coords_hbm, coords_ref), (waves_hbm, waves_ref)]
        )
    ]
    for load in loads:
        load.start()
    blocks = waves_ref.shape[0]
    out_ref[...] = jnp.zeros_like(out_ref)
    offset = (lax.broadcasted_iota(jnp.int32, (SUB, ROWS), 0) - SUB // 2).astype(jnp.float32) * (1.0 / SUB)
    square = offset * offset
    side = lax.broadcasted_iota(jnp.int32, (SUB, 4 * SUB), 1) // (2 * SUB)
    live = live_ref[0]
    for load in loads:
        load.wait()

    def picture(block):
        first, second, third = [coords_ref[axis, pl.ds(block, 1), :] for axis in range(3)]
        waves = waves_ref[block] * (block < live).astype(jnp.float32)
        depth = third * square
        turns_first = first * offset + depth
        turns_second = second * offset + depth
        layers = []
        for channel in range(CH):
            factor = scale_ref[channel]
            sine, cosine = sincos_turns(turns_first * factor)
            real, imag = waves[2 * channel:2 * channel + 1, :], waves[2 * channel + 1:2 * channel + 2, :]
            left_high, left_low = split(
                jnp.concatenate([real * cosine - imag * sine, real * sine + imag * cosine], axis=1)
            )
            sine, cosine = sincos_turns(turns_second * factor)
            sine_high, sine_low = split(sine)
            cosine_high, cosine_low = split(cosine)
            right = jnp.concatenate(
                [
                    jnp.concatenate([cosine_high, -sine_high], axis=1),
                    jnp.concatenate([sine_high, cosine_high], axis=1),
                    jnp.concatenate([cosine_low, -sine_low], axis=1),
                    jnp.concatenate([sine_low, cosine_low], axis=1),
                ],
                axis=0,
            )
            product = dot_nt(jnp.concatenate([left_high, left_low], axis=0), right)
            product = product[:SUB] + product[SUB:]
            layers.append(product + pltpu.roll(product, 2 * SUB, 1))
        return layers

    def body(step, carry):
        base = step * UNROLL
        group = [picture(base + k) for k in range(UNROLL)]
        for k in range(UNROLL):
            label = labels_ref[base + k]
            mask = side == (label & 1)
            for channel in range(CH):
                out_ref[channel, label >> 1] += jnp.where(mask, group[k][channel], 0.0)
        return carry

    lax.fori_loop(0, blocks // UNROLL, body, 0)


def partial_pictures(coords, waves, labels, live, scale, subgrids):
    smem = pl.BlockSpec(memory_space=pltpu.SMEM)
    hbm = pl.BlockSpec(memory_space=pltpu.HBM)
    return pl.pallas_call(
        pictures_kernel,
        out_shape=jax.ShapeDtypeStruct((CH, subgrids // 2, SUB, 4 * SUB), jnp.float32),
        in_specs=[hbm, smem, smem, hbm, hbm],
        out_specs=pl.BlockSpec(memory_space=pltpu.VMEM),
        scratch_shapes=[
            pltpu.SMEM(labels.shape, jnp.int32),
            pltpu.VMEM(coords.shape, jnp.float32),
            pltpu.VMEM(waves.shape, jnp.float32),
            pltpu.SemaphoreType.DMA((3,)),
        ],
        compiler_params=pltpu.CompilerParams(vmem_limit_bytes=32 * 1024 * 1024),
        name="block_pictures",
    )(labels, live, scale, coords, waves)


def transform_matrices():
    at = np.arange(SUB)
    taper = np.sin(np.pi * (at + 0.5) / SUB) ** 2
    angles = 2.0 * math.pi * (at[:, None] * at[None, :] % SUB) / SUB
    real, imag = taper[:, None] * np.cos(angles), -taper[:, None] * np.sin(angles)
    plain = np.block([[real, imag], [-imag, real]])
    turned = np.block([[-imag, real], [-real, -imag]])
    columns = np.concatenate([np.kron(np.eye(2), plain), np.kron(np.eye(2), turned)], axis=1)
    rows = np.concatenate([real.T, imag.T], axis=1) / (ROWS * SUB)
    return columns.astype(np.float32), rows.astype(np.float32)


def stage_shapes(workers):
    bits = workers.bit_length() - 1
    return [[0] * bits, [0] + [bits - 1 - step for step in range(1, bits)]]


def combine_kernel(workers, tiles, *refs):
    corners_ref, data_ref, columns_ref, rows_ref, out_ref = refs[:5]
    bits = workers.bit_length() - 1
    orders = stage_shapes(workers)
    scratch = list(refs[5:])
    received = [[scratch.pop(0) for _ in range(bits)] for _ in range(2)]
    kept = [[scratch.pop(0) for _ in range(bits)] for _ in range(2)]
    placed, outgoing, incoming, send_sem, recv_sem, tile_send, tile_recv = scratch
    worker, tile = lax.axis_index("work"), lax.axis_index("tile")
    height = out_ref.shape[1]

    def partner(bit):
        return worker + (1 << bit) * (1 - 2 * ((worker >> bit) & 1))

    barrier = pltpu.get_barrier_semaphore()
    for bit in range(bits):
        pl.semaphore_signal(barrier, inc=1, device_id=(partner(bit), tile), device_id_type=MESH)
    for far in range(1, tiles):
        pl.semaphore_signal(barrier, inc=1, device_id=(worker, lax.rem(tile + far, tiles)), device_id_type=MESH)
    pl.semaphore_wait(barrier, bits + tiles - 1)

    def own_part(channel, half, step):
        if step == 0:
            return data_ref.at[channel], pl.ds(half * QUARTER, QUARTER)
        return kept[half][step - 1].at[channel], slice(None)

    def halved_bit(half, step):
        return 0 if step == 0 else (step if half == 0 else bits - step)

    def step_copy(channel, half, step):
        bit = halved_bit(half, step)
        source, pairs = own_part(channel, half, step)
        return pltpu.make_async_remote_copy(
            src_ref=source.at[:, 1 - ((worker >> bit) & 1), :, pairs],
            dst_ref=received[half][step].at[channel],
            send_sem=send_sem.at[channel, half, step],
            recv_sem=recv_sem.at[channel, half, step],
            device_id=(partner(bit), tile),
            device_id_type=MESH,
        )

    def step_sum(channel, half, step):
        mine = (worker >> halved_bit(half, step)) & 1
        source, pairs = own_part(channel, half, step)
        arrived = received[half][step].at[channel]
        target = kept[half][step].at[channel]
        if step == bits - 1:
            target[...] = source[0, mine, 0, pairs] + arrived[0, 0]
            return
        low, low_next = arrived.shape[1], target.shape[2]
        for a in range(arrived.shape[0]):
            for b in range(low):
                at = a * low + b
                target[at // (2 * low_next), at // low_next % 2, at % low_next] = source[a, mine, b, pairs] + arrived[a, b]

    copies = {}

    def advance(channel, step):
        for half in range(2):
            copies[channel, half].wait()
            step_sum(channel, half, step)
            if step < bits - 1:
                copies[channel, half] = step_copy(channel, half, step + 1)
                copies[channel, half].start()

    width = 4 * SUB
    columns, rows = columns_ref[...], rows_ref[...]
    lane = lax.broadcasted_iota(jnp.int32, (1, SUBW * SUB), 1)
    row_at = lane % SUB
    for s in range(SUBW):
        row_at = row_at + jnp.where(lane // SUB == s, corners_ref[0, worker * SUBW + s], 0)
    stripe = lax.broadcasted_iota(jnp.int32, (width, GCW), 0)
    across = lax.broadcasted_iota(jnp.int32, (width, GCW), 1) - stripe % SUB
    group = lax.broadcasted_iota(jnp.int32, (width, width), 0) // SUB
    same = group == lax.broadcasted_iota(jnp.int32, (width, width), 1) // SUB

    def transform(channel):
        pictures = jnp.concatenate(
            [kept[half][bits - 1][channel].reshape(QUARTER * SUB, width) for half in range(2)], axis=0
        )
        first = jnp.dot(pictures, columns, precision=highest, preferred_element_type=jnp.float32)
        pieces = [first[j * SUB:(j + 1) * SUB] for j in range(2 * QUARTER)]
        stacked = jnp.concatenate(
            [jnp.concatenate([piece[:, at:at + width] for piece in pieces], axis=1) for at in (0, width)], axis=0
        )
        spectra = jnp.dot(rows, stacked, precision=highest, preferred_element_type=jnp.float32)
        for j in range(2 * QUARTER):
            spectrum = spectra[:, j * width:(j + 1) * width]
            spread = jnp.where(same, jnp.concatenate([spectrum] * 4, axis=0), 0.0)
            high, low = split(spread)
            column = [corners_ref[1, worker * SUBW + 2 * j + side] - worker * GCW for side in range(2)]
            target = across == jnp.where(stripe < 2 * SUB, column[0], column[1])
            target = jnp.where(target, 1.0, 0.0).astype(jnp.bfloat16)
            wide = jnp.dot(jnp.concatenate([high, low], axis=0), target, preferred_element_type=jnp.float32)
            high, low = split(wide[:width] + wide[width:])
            for side in range(2):
                for part in range(2):
                    here = slice((2 * side + part) * SUB, (2 * side + part + 1) * SUB)
                    there = slice((2 * j + side) * SUB, (2 * j + side + 1) * SUB)
                    placed[2 * channel + part, there, :GCW] = high[here]
                    placed[2 * channel + part, there, GCW:] = low[here]

    def tile_rows(channel, which, store):
        line = lax.broadcasted_iota(jnp.int32, (height, SUBW * SUB), 0) + which * height
        select = jnp.where(line == row_at, 1.0, 0.0).astype(jnp.bfloat16)
        for part in range(2):
            both = jnp.dot(select, placed[2 * channel + part], preferred_element_type=jnp.float32)
            store[part] = both[:, :GCW] + both[:, GCW:]

    sent = []

    def spread_tiles(channel):
        for far in range(tiles - 1, 0, -1):
            which = lax.rem(tile + far, tiles)
            tile_rows(channel, which, outgoing.at[channel, far - 1])
            copy = pltpu.make_async_remote_copy(
                src_ref=outgoing.at[channel, far - 1],
                dst_ref=incoming.at[channel, far - 1],
                send_sem=tile_send.at[channel, far - 1],
                recv_sem=tile_recv.at[channel, far - 1],
                device_id=(worker, which),
                device_id_type=MESH,
            )
            copy.start()
            sent.append(copy)
        tile_rows(channel, tile, out_ref.at[pl.ds(2 * channel, 2)])

    for channel in range(CH):
        for half in range(2):
            copies[channel, half] = step_copy(channel, half, 0)
            copies[channel, half].start()
    for step in range(bits):
        advance(0, step)
        if 1 <= step <= bits - 2:
            advance(1, step - 1)
    transform(0)
    advance(1, bits - 2)
    spread_tiles(0)
    advance(1, bits - 1)
    transform(1)
    spread_tiles(1)
    for copy in sent:
        copy.wait()
    for channel in range(CH):
        total = out_ref[2 * channel:2 * channel + 2]
        for far in range(tiles - 1):
            total = total + incoming[channel, far]
        out_ref[2 * channel:2 * channel + 2] = total


def combine(pictures, corners, workers, tiles, height):
    bits = workers.bit_length() - 1
    received, kept = [], []
    tail = (QUARTER, SUB, 4 * SUB)
    for order in stage_shapes(workers):
        for step in range(bits):
            count = workers >> step
            low = 1 << order[step]
            received.append(pltpu.VMEM((CH, count // (2 * low), low) + tail, jnp.float32))
            if step < bits - 1:
                low = 1 << order[step + 1]
                kept.append(pltpu.VMEM((CH, count // 2 // (2 * low), 2, low) + tail, jnp.float32))
            else:
                kept.append(pltpu.VMEM((CH,) + tail, jnp.float32))
    columns, rows = transform_matrices()
    vmem = pl.BlockSpec(memory_space=pltpu.VMEM)
    return pl.pallas_call(
        functools.partial(combine_kernel, workers, tiles),
        out_shape=jax.ShapeDtypeStruct((2 * CH, height, GCW), jnp.float32),
        in_specs=[pl.BlockSpec(memory_space=pltpu.SMEM), vmem, vmem, vmem],
        out_specs=vmem,
        scratch_shapes=received + kept + [
            pltpu.VMEM((2 * CH, SUBW * SUB, 2 * GCW), jnp.bfloat16),
            pltpu.VMEM((CH, tiles - 1, 2, height, GCW), jnp.float32),
            pltpu.VMEM((CH, tiles - 1, 2, height, GCW), jnp.float32),
            pltpu.SemaphoreType.DMA((CH, 2, bits)),
            pltpu.SemaphoreType.DMA((CH, 2, bits)),
            pltpu.SemaphoreType.DMA((CH, tiles - 1)),
            pltpu.SemaphoreType.DMA((CH, tiles - 1)),
        ],
        compiler_params=pltpu.CompilerParams(
            collective_id=0, has_side_effects=True, vmem_limit_bytes=48 * 1024 * 1024
        ),
        name="reduce_and_place",
    )(
        jnp.transpose(corners),
        pictures.reshape(CH, workers // 2, 2, 1, 2 * QUARTER, SUB, 4 * SUB),
        jnp.asarray(columns),
        jnp.asarray(rows),
    )


def local(height, block_coords, block_visibilities, subgrid_of_block, live_blocks, corners, channel_scale):
    workers = lax.axis_size("work")
    tiles = lax.axis_size("tile")
    pictures = partial_pictures(
        jnp.transpose(block_coords, (1, 0, 2)), block_visibilities, subgrid_of_block, live_blocks, channel_scale, corners.shape[0]
    )
    return combine(pictures, corners, workers, tiles, height)


def solution(mesh):
    height = 64
    return jax.shard_map(
        functools.partial(local, height),
        mesh=mesh,
        in_specs=(
            P(("work", "tile"), None, None),
            P(("work", "tile"), None, None),
            P(("work", "tile")),
            P(("work", "tile")),
            P(),
            P(),
        ),
        out_specs=P(None, "tile", "work"),
        check_vma=False,
    )
```

time: 60.7 us -> 53.7 us (0.88)
  Pallas kernels: 55.7 us -> 49 us
    pallas_call x1, Pallas kernels: 38.3 us -> 31.7 us  [combine(): pl.pallas_call(functools.partial(combine_kernel, workers, tiles), out_sha...]
where the time goes in v2:
time: 53.7 us; the launch traced here: 53.5 us
  Pallas kernels  49 us (91%)
  local copies, waits for them, and re-layouts  3.85 us (7%)
  between operations  0.72 us (1%)
    pallas_call x1, Pallas kernels, combine(): pl.pallas_call(functools.partial(combine_kernel, workers, tiles), out_sha...  31.7 us
    pallas_call x1, Pallas kernels, partial_pictures(): pl.pallas_call(pictures_kernel, out_shape=jax.ShapeDtypeStruct((CH, subgr...  17.3 us
    unnamed x15, local copies, waits for them, and re-layouts  3.85 us

profile of v2, /device:TPU:0, one launch (start us, length us, event | category | flops | bytes accessed | tf_op | source)
XLA Modules:
  0.0 53.5 jit_solution(11373195760842639813)
XLA Ops:
  0.0 0.0 copy-start.4
  0.7 0.0 copy-start
  0.7 0.9 %copy-done = f32[128,4,128]{2,1,0:T(4,128)S(1)} copy-done((f32[128,4,128]{2,1,0:T(4,128)S(1)}, f32[128,4,128]{2,1,0:T(4,128)}, u32[]{:S(2)}) %copy-start) | copy-done | bytes 262168
  1.6 0.0 copy-start.1
  1.6 0.9 %copy-done.1 = f32[128,3,128]{2,0,1:T(8,128)S(1)} copy-done((f32[128,3,128]{2,0,1:T(8,128)S(1)}, f32[128,3,128]{2,0,1:T(8,128)}, u32[]{:S(2)}) %copy-start.1) | copy-done | bytes 196632
  2.5 0.0 copy-start.5
  2.5 0.7 %copy-done.5 = s32[128]{0:T(128)S(1)} copy-done((s32[128]{0:T(128)S(1)}, s32[128]{0:T(128)}, u32[]{:S(2)}) %copy-start.5) | copy-done | bytes 536
  3.2 0.0 copy-start.6
  3.2 0.7 %copy-done.6 = f32[2]{0:T(128)S(1)} copy-done((f32[2]{0:T(128)S(1)}, f32[2]{0:T(128)}, u32[]{:S(2)}) %copy-start.6) | copy-done | bytes 32
  3.9 0.0 copy-start.2
  3.9 0.0 copy-start.3
  3.9 17.3 %block_pictures.1 = f32[2,64,32,128]{3,2,1,0:T(8,128)S(1)} custom-call(s32[128]{0:T(128)S(1)} %copy-done.5, s32[1]{0:T(128)S(6)} %copy.10.live_ref, f32[2]{0:T(128)S(1)} %copy-done.6, f32[3,128,128]{2,1,0:T(8,128)S(1)} %bitcast.4, f32[128,4,128]{2,1,0:T(4,128)S(1)} %copy-done), custom_call_target="tpu_custom_call" | custom-call | tf_op jit(solution)/shard_map/block_pictures/pallas_call | solution.py:113
  21.2 0.0 copy-done.4
  21.2 0.0 copy-done.2
  21.2 0.0 copy-done.3
  21.2 31.7 %reduce_and_place.1 = f32[4,64,128]{2,1,0:T(8,128)S(1)} custom-call(s32[2,128]{1,0:T(2,128)S(1)} %bitcast.5, f32[2,4,2,1,8,32,128]{6,5,4,3,2,1,0:T(8,128)S(1)} %bitcast.3, f32[128,256]{1,0:T(8,128)S(1)} %copy-done.2, f32[32,64]{1,0:T(8,128)S(1)} %copy-done.3), custom_call_target="tpu_custom_call" | custom-call | tf_op jit(solution)/shard_map/reduce_and_place/pallas_call | solution.py:312
  52.9 0.7 %copy.11 = f32[4,64,128]{2,1,0:T(8,128)} copy(f32[4,64,128]{2,1,0:T(8,128)S(1)} %reduce_and_place.1) | data formatting | bytes 262144
Async XLA Ops:
  0.0 21.2 %copy-start.4 = (s32[128,2]{0,1:T(2,128)S(1)}, s32[128,2]{0,1:T(2,128)}, u32[]{:S(2)}) copy-start(s32[128,2]{0,1:T(2,128)} %param.12) | copy-start | bytes 3076
  0.7 1.0 %copy-start = (f32[128,4,128]{2,1,0:T(4,128)S(1)}, f32[128,4,128]{2,1,0:T(4,128)}, u32[]{:S(2)}) copy-start(f32[128,4,128]{2,1,0:T(4,128)} %waves_hbm.1) | copy-start | bytes 786436
  1.6 0.9 %copy-start.1 = (f32[128,3,128]{2,0,1:T(8,128)S(1)}, f32[128,3,128]{2,0,1:T(8,128)}, u32[]{:S(2)}) copy-start(f32[128,3,128]{2,0,1:T(8,128)} %param.8) | copy-start | bytes 589828
  2.5 0.7 %copy-start.5 = (s32[128]{0:T(128)S(1)}, s32[128]{0:T(128)}, u32[]{:S(2)}) copy-start(s32[128]{0:T(128)} %labels_hbm.1) | copy-start | bytes 1540
  3.2 0.7 %copy-start.6 = (f32[2]{0:T(128)S(1)}, f32[2]{0:T(128)}, u32[]{:S(2)}) copy-start(f32[2]{0:T(128)} %scale_ref.1) | copy-start | bytes 28
  3.9 17.3 %copy-start.2 = (f32[128,256]{1,0:T(8,128)S(1)}, f32[128,256]{1,0:T(8,128)}, u32[]{:S(2)}) copy-start(f32[128,256]{1,0:T(8,128)} %constant.4.clone.refs_2_) | copy-start | bytes 393220
  3.9 17.3 %copy-start.3 = (f32[32,64]{1,0:T(8,128)S(1)}, f32[32,64]{1,0:T(8,128)}, u32[]{:S(2)}) copy-start(f32[32,64]{1,0:T(8,128)} %constant.5.clone.refs_3_) | copy-start | bytes 24580

commit v3 on v2

v3 whole, which is shorter than its diff:
```python
import functools
import math

import jax
import jax.numpy as jnp
import numpy as np
from jax import lax
from jax.experimental import pallas as pl
from jax.experimental.pallas import tpu as pltpu
from jax.sharding import PartitionSpec as P

CH = 2
SUB = 32
ROWS = 128
GCW = 128
SUBW = 16
FOLD = SUB // 2
HALF = FOLD // 2
UNROLL = 4
MESH = pl.DeviceIdType.MESH
highest = lax.Precision.HIGHEST

NEAREST = 12582912.0
SIN = (6.283184916495431, -41.34158923268848, 81.59994332978006, -76.61447253122435, 41.34288235446963, -12.471243534886277)
COS = (0.9999992107823215, -19.73898035576396, 64.92865742103214, -85.2716215342875, 58.7904921200778, -21.07110562755528)


def horner(coefficients, z):
    total = jnp.full_like(z, coefficients[-1])
    for value in coefficients[-2::-1]:
        total = total * z + value
    return total


def sincos_turns(turns):
    rest = turns - ((turns + NEAREST) - NEAREST)
    z = rest * rest
    return rest * horner(SIN, z), horner(COS, z)


def split(value):
    high = value.astype(jnp.bfloat16)
    return high, (value - high.astype(jnp.float32)).astype(jnp.bfloat16)


def dot_nt(left, right):
    return lax.dot_general(left, right, (((1,), (1,)), ((), ())), preferred_element_type=jnp.float32)


def transform_matrices():
    at = np.arange(SUB)
    taper = np.sin(np.pi * (at + 0.5) / SUB) ** 2
    angles = 2.0 * math.pi * (at[:, None] * at[None, :] % SUB) / SUB
    real, imag = taper[:, None] * np.cos(angles), -taper[:, None] * np.sin(angles)
    plain = np.block([[real, imag], [-imag, real]])
    turned = np.block([[-imag, real], [-real, -imag]])
    columns = np.kron(np.eye(2), np.concatenate([plain, turned], axis=1))
    rows = np.concatenate([real.T, imag.T], axis=1) / (ROWS * SUB)
    return columns.astype(np.float32), rows.astype(np.float32)


def stage_shapes(workers):
    bits = workers.bit_length() - 1
    return [[0] * bits, [0] + [bits - 1 - step for step in range(1, bits)]]


def grid_kernel(workers, tiles, *refs):
    live_ref, scale_ref, corners_ref, labels_ref, coords_ref, waves_ref, columns_ref, rows_ref, out_ref = refs[:9]
    bits = workers.bit_length() - 1
    orders = stage_shapes(workers)
    scratch = list(refs[9:])
    received = [[scratch.pop(0) for _ in range(bits)] for _ in range(2)]
    kept = [[scratch.pop(0) for _ in range(bits)] for _ in range(2)]
    pictures_ref, data_ref, first_ref, placed, outgoing, incoming, send_sem, recv_sem, tile_send, tile_recv = scratch
    worker, tile = lax.axis_index("work"), lax.axis_index("tile")
    height = out_ref.shape[1]

    def partner(bit):
        return worker + (1 << bit) * (1 - 2 * ((worker >> bit) & 1))

    barrier = pltpu.get_barrier_semaphore()
    for bit in range(bits):
        pl.semaphore_signal(barrier, inc=1, device_id=(partner(bit), tile), device_id_type=MESH)
    for far in range(1, tiles):
        pl.semaphore_signal(barrier, inc=1, device_id=(worker, lax.rem(tile + far, tiles)), device_id_type=MESH)

    def own_part(channel, half, step):
        if step == 0:
            return data_ref.at[channel], pl.ds(half * HALF, HALF)
        return kept[half][step - 1].at[channel], slice(None)

    def halved_bit(half, step):
        return 0 if step == 0 else (step if half == 0 else bits - step)

    def step_copy(channel, half, step):
        bit = halved_bit(half, step)
        source, pairs = own_part(channel, half, step)
        return pltpu.make_async_remote_copy(
            src_ref=source.at[:, 1 - ((worker >> bit) & 1), :, pairs],
            dst_ref=received[half][step].at[channel],
            send_sem=send_sem.at[channel, half, step],
            recv_sem=recv_sem.at[channel, half, step],
            device_id=(partner(bit), tile),
            device_id_type=MESH,
        )

    def step_sum(channel, half, step):
        mine = (worker >> halved_bit(half, step)) & 1
        source, pairs = own_part(channel, half, step)
        arrived = received[half][step].at[channel]
        target = kept[half][step].at[channel]
        if step == bits - 1:
            target[...] = source[0, mine, 0, pairs] + arrived[0, 0]
            return
        low, low_next = arrived.shape[1], target.shape[2]
        for a in range(arrived.shape[0]):
            for b in range(low):
                at = a * low + b
                target[at // (2 * low_next), at // low_next % 2, at % low_next] = source[a, mine, b, pairs] + arrived[a, b]

    copies = {}

    def advance(channel, step):
        for half in range(2):
            copies[channel, half].wait()
            step_sum(channel, half, step)
            if step < bits - 1:
                copies[channel, half] = step_copy(channel, half, step + 1)
                copies[channel, half].start()

    width = 4 * SUB
    columns, rows = columns_ref[...], rows_ref[...]
    lane = lax.broadcasted_iota(jnp.int32, (1, SUBW * SUB), 1)
    row_at = lane % SUB
    for s in range(SUBW):
        row_at = row_at + jnp.where(lane // SUB == s, corners_ref[0, worker * SUBW + s], 0)
    stripe = lax.broadcasted_iota(jnp.int32, (width, GCW), 0)
    across = lax.broadcasted_iota(jnp.int32, (width, GCW), 1) - stripe % SUB
    group = lax.broadcasted_iota(jnp.int32, (width, width), 0) // SUB
    same = group == lax.broadcasted_iota(jnp.int32, (width, width), 1) // SUB

    low_lanes = lax.broadcasted_iota(jnp.int32, (SUB, width), 1) < 2 * SUB

    def transform(channel):
        pictures = jnp.concatenate(
            [kept[half][bits - 1][channel].reshape(HALF * SUBW, width) for half in range(2)], axis=0
        )
        first = jnp.dot(pictures, columns, precision=highest, preferred_element_type=jnp.float32)
        first_ref[0] = first[:, :width]
        first_ref[1] = first[:, width:]
        plain, turned = [], []
        for j in range(SUBW // 2):
            even, odd = [
                jnp.concatenate(
                    [first_ref[side, pl.ds(2 * j + s, FOLD, stride=SUBW), :] for side in range(2)], axis=0
                )
                for s in range(2)
            ]
            plain.append(jnp.where(low_lanes, even, pltpu.roll(odd, 2 * SUB, 1)))
            turned.append(jnp.where(low_lanes, pltpu.roll(even, 2 * SUB, 1), odd))
        stacked = jnp.concatenate([jnp.concatenate(plain, axis=1), jnp.concatenate(turned, axis=1)], axis=0)
        spectra = jnp.dot(rows, stacked, precision=highest, preferred_element_type=jnp.float32)
        for j in range(SUBW // 2):
            spectrum = spectra[:, j * width:(j + 1) * width]
            spread = jnp.where(same, jnp.concatenate([spectrum] * 4, axis=0), 0.0)
            high, low = split(spread)
            column = [corners_ref[1, worker * SUBW + 2 * j + side] - worker * GCW for side in range(2)]
            target = across == jnp.where(stripe < 2 * SUB, column[0], column[1])
            target = jnp.where(target, 1.0, 0.0).astype(jnp.bfloat16)
            wide = jnp.dot(jnp.concatenate([high, low], axis=0), target, preferred_element_type=jnp.float32)
            high, low = split(wide[:width] + wide[width:])
            for side in range(2):
                for part in range(2):
                    here = slice((2 * side + part) * SUB, (2 * side + part + 1) * SUB)
                    there = slice((2 * j + side) * SUB, (2 * j + side + 1) * SUB)
                    placed[2 * channel + part, there, :GCW] = high[here]
                    placed[2 * channel + part, there, GCW:] = low[here]

    def tile_rows(channel, which, store):
        line = lax.broadcasted_iota(jnp.int32, (height, SUBW * SUB), 0) + which * height
        select = jnp.where(line == row_at, 1.0, 0.0).astype(jnp.bfloat16)
        for part in range(2):
            both = jnp.dot(select, placed[2 * channel + part], preferred_element_type=jnp.float32)
            store[part] = both[:, :GCW] + both[:, GCW:]

    blocks = waves_ref.shape[0]
    steps = blocks // UNROLL
    offset = (lax.broadcasted_iota(jnp.int32, (SUB, ROWS), 0) - SUB // 2).astype(jnp.float32) * (1.0 / SUB)
    square = offset * offset
    low_half = lax.broadcasted_iota(jnp.int32, (FOLD, width), 1) < 2 * SUB

    def picture(channel, block):
        first, second, third = [coords_ref[axis, pl.ds(block, 1), :] for axis in range(3)]
        waves = waves_ref[block]
        factor = scale_ref[channel]
        depth = third * square
        sine, cosine = sincos_turns((first * offset + depth) * factor)
        real, imag = waves[2 * channel:2 * channel + 1, :], waves[2 * channel + 1:2 * channel + 2, :]
        left_high, left_low = split(
            jnp.concatenate([real * cosine - imag * sine, real * sine + imag * cosine], axis=1)
        )
        sine, cosine = sincos_turns((second * offset + depth) * factor)
        sine_high, sine_low = split(sine)
        cosine_high, cosine_low = split(cosine)
        right = jnp.concatenate(
            [
                jnp.concatenate([cosine_high, -sine_high], axis=1),
                jnp.concatenate([sine_high, cosine_high], axis=1),
                jnp.concatenate([cosine_low, -sine_low], axis=1),
                jnp.concatenate([sine_low, cosine_low], axis=1),
            ],
            axis=0,
        )
        product = dot_nt(jnp.concatenate([left_high, left_low], axis=0), right)
        product = product[:SUB] + product[SUB:]
        product = product + pltpu.roll(product, 2 * SUB, 1)
        return jnp.where(low_half, product[:FOLD], product[FOLD:])

    def fill(channel, begin, end):
        def body(step, carry):
            base = step * UNROLL
            group = [picture(channel, base + k) for k in range(UNROLL)]
            for k in range(UNROLL):
                pictures_ref[pl.ds(base + k, FOLD, stride=blocks), :] = group[k]
            return carry

        lax.fori_loop(begin, end, body, 0)

    def merge(channel):
        subgrids = SUBW * workers
        named = lax.broadcasted_iota(jnp.int32, (subgrids, blocks), 0) == labels_ref[...]
        alive = lax.broadcasted_iota(jnp.int32, (subgrids, blocks), 1) < live_ref[0]
        choose = jnp.where(named & alive, 1.0, 0.0).astype(jnp.bfloat16)
        for x in range(FOLD):
            high, low = split(pictures_ref[x * blocks:(x + 1) * blocks])
            both = jnp.dot(choose, jnp.concatenate([high, low], axis=1), preferred_element_type=jnp.float32)
            both = both[:, :width] + both[:, width:]
            for w in range(workers):
                data_ref[channel, w // 2, w % 2, 0, x] = both[w * SUBW:(w + 1) * SUBW]

    def begin(channel):
        for half in range(2):
            copies[channel, half] = step_copy(channel, half, 0)
            copies[channel, half].start()

    sent = []

    def spread_tiles(channel):
        for far in range(tiles - 1, 0, -1):
            which = lax.rem(tile + far, tiles)
            tile_rows(channel, which, outgoing.at[channel, far - 1])
            copy = pltpu.make_async_remote_copy(
                src_ref=outgoing.at[channel, far - 1],
                dst_ref=incoming.at[channel, far - 1],
                send_sem=tile_send.at[channel, far - 1],
                recv_sem=tile_recv.at[channel, far - 1],
                device_id=(worker, which),
                device_id_type=MESH,
            )
            copy.start()
            sent.append(copy)
        tile_rows(channel, tile, out_ref.at[pl.ds(2 * channel, 2)])

    fill(0, 0, steps)
    merge(0)
    pl.semaphore_wait(barrier, bits + tiles - 1)
    begin(0)
    done = 0
    for step in range(bits):
        until = steps * (2 * step + 1) // (2 * bits + 1)
        fill(1, done, until)
        done = until
        advance(0, step)
    transform(0)
    spread_tiles(0)
    fill(1, done, steps)
    merge(1)
    begin(1)
    for step in range(bits):
        advance(1, step)
    transform(1)
    spread_tiles(1)
    for copy in sent:
        copy.wait()
    for channel in range(CH):
        total = out_ref[2 * channel:2 * channel + 2]
        for far in range(tiles - 1):
            total = total + incoming[channel, far]
        out_ref[2 * channel:2 * channel + 2] = total


def gridded(coords, waves, labels, live, corners, scale, workers, tiles, height):
    bits = workers.bit_length() - 1
    blocks = waves.shape[0]
    width = 4 * SUB
    received, kept = [], []
    tail = (HALF, SUBW, width)
    for order in stage_shapes(workers):
        for step in range(bits):
            count = workers >> step
            low = 1 << order[step]
            received.append(pltpu.VMEM((CH, count // (2 * low), low) + tail, jnp.float32))
            if step < bits - 1:
                low = 1 << order[step + 1]
                kept.append(pltpu.VMEM((CH, count // 2 // (2 * low), 2, low) + tail, jnp.float32))
            else:
                kept.append(pltpu.VMEM((CH,) + tail, jnp.float32))
    columns, rows = transform_matrices()
    vmem = pl.BlockSpec(memory_space=pltpu.VMEM)
    smem = pl.BlockSpec(memory_space=pltpu.SMEM)
    return pl.pallas_call(
        functools.partial(grid_kernel, workers, tiles),
        out_shape=jax.ShapeDtypeStruct((2 * CH, height, GCW), jnp.float32),
        in_specs=[smem, smem, smem, vmem, vmem, vmem, vmem, vmem],
        out_specs=vmem,
        scratch_shapes=received + kept + [
            pltpu.VMEM((FOLD * blocks, width), jnp.float32),
            pltpu.VMEM((CH, workers // 2, 2, 1, FOLD, SUBW, width), jnp.float32),
            pltpu.VMEM((2, FOLD * SUBW, width), jnp.float32),
            pltpu.VMEM((2 * CH, SUBW * SUB, 2 * GCW), jnp.bfloat16),
            pltpu.VMEM((CH, tiles - 1, 2, height, GCW), jnp.float32),
            pltpu.VMEM((CH, tiles - 1, 2, height, GCW), jnp.float32),
            pltpu.SemaphoreType.DMA((CH, 2, bits)),
            pltpu.SemaphoreType.DMA((CH, 2, bits)),
            pltpu.SemaphoreType.DMA((CH, tiles - 1)),
            pltpu.SemaphoreType.DMA((CH, tiles - 1)),
        ],
        compiler_params=pltpu.CompilerParams(
            collective_id=0, has_side_effects=True, vmem_limit_bytes=56 * 1024 * 1024
        ),
        name="grid_blocks",
    )(live, scale, jnp.transpose(corners), labels.reshape(1, blocks), coords, waves, jnp.asarray(columns), jnp.asarray(rows))


def local(height, block_coords, block_visibilities, subgrid_of_block, live_blocks, corners, channel_scale):
    workers = lax.axis_size("work")
    tiles = lax.axis_size("tile")
    return gridded(
        jnp.transpose(block_coords, (1, 0, 2)), block_visibilities, subgrid_of_block, live_blocks, corners,
        channel_scale, workers, tiles, height,
    )


def solution(mesh):
    height = 64
    return jax.shard_map(
        functools.partial(local, height),
        mesh=mesh,
        in_specs=(
            P(("work", "tile"), None, None),
            P(("work", "tile"), None, None),
            P(("work", "tile")),
            P(("work", "tile")),
            P(),
            P(),
        ),
        out_specs=P(None, "tile", "work"),
        check_vma=False,
    )
```

time: 53.7 us -> 54.3 us (1.011)
  Pallas kernels: 49 us -> 52 us
  local copies, waits for them, and re-layouts: 3.85 us -> 1.57 us
    pallas_call x2 -> x1, Pallas kernels: 49 us -> 52 us  [gridded(): pl.pallas_call(functools.partial(grid_kernel, workers, tiles), out_shape=...]
    unnamed x15 -> x1, local copies, waits for them, and re-layouts: 3.85 us -> 1.57 us
where the time goes in v3:
time: 54.3 us; the launch traced here: 54.2 us
  Pallas kernels  52 us (96%)
  local copies, waits for them, and re-layouts  1.57 us (3%)
  between operations  0.66 us (1%)
    pallas_call x1, Pallas kernels, gridded(): pl.pallas_call(functools.partial(grid_kernel, workers, tiles), out_shape=...  52 us
    unnamed x1, local copies, waits for them, and re-layouts  1.57 us

profile of v3, /device:TPU:0, one launch (start us, length us, event | category | flops | bytes accessed | tf_op | source)
XLA Modules:
  0.0 54.2 jit_solution(650902495601178369)
XLA Ops:
  0.7 52.0 %grid_blocks.1 = f32[4,64,128]{2,1,0:T(8,128)} custom-call(s32[1]{0:T(128)S(6)} %copy.10.refs_0_, f32[2]{0:T(128)} %refs_1_.1, s32[2,128]{1,0:T(2,128)} %bitcast.4, s32[1,128]{1,0:T(1,128)} %bitcast.5, f32[3,128,128]{2,1,0:T(8,128)} %bitcast.3, f32[128,4,128]{2,1,0:T(4,128)} %refs_5_.1, f32[128,256]{1,0:T(8,128)} %constant.4.clone.refs_6_, ...), custom_call_target="tpu_custom_call" | custom-call | tf_op jit(solution)/shard_map/grid_blocks/pallas_call | solution.py:311
  52.6 1.6 %copy.11 = f32[4,64,128]{2,1,0:T(8,128)} copy(f32[4,64,128]{2,1,0:T(8,128)} %grid_blocks.1) | data formatting | bytes 262144

commit v4 on v3

--- a/solution.py
+++ b/solution.py
@@ -16,7 +16,7 @@
 SUBW = 16
 FOLD = SUB // 2
 HALF = FOLD // 2
-UNROLL = 4
+UNROLL = 16
 MESH = pl.DeviceIdType.MESH
 highest = lax.Precision.HIGHEST
 
@@ -267,7 +267,7 @@
     begin(0)
     done = 0
     for step in range(bits):
-        until = steps * (2 * step + 1) // (2 * bits + 1)
+        until = steps - (4 * steps // 5 >> step)
         fill(1, done, until)
         done = until
         advance(0, step)

time: 54.3 us -> 46.9 us (0.86)
  Pallas kernels: 52 us -> 44.5 us
    pallas_call x1, Pallas kernels: 52 us -> 44.5 us  [gridded(): pl.pallas_call(functools.partial(grid_kernel, workers, tiles), out_shape=...]
where the time goes in v4:
time: 46.9 us; the launch traced here: 46.7 us
  Pallas kernels  44.5 us (95%)
  local copies, waits for them, and re-layouts  1.57 us (3%)
  between operations  0.66 us (1%)
    pallas_call x1, Pallas kernels, gridded(): pl.pallas_call(functools.partial(grid_kernel, workers, tiles), out_shape=...  44.5 us
    unnamed x1, local copies, waits for them, and re-layouts  1.57 us

profile of v4, /device:TPU:0, one launch (start us, length us, event | category | flops | bytes accessed | tf_op | source)
XLA Modules:
  0.0 46.7 jit_solution(11808652254421371815)
XLA Ops:
  0.7 44.5 %grid_blocks.1 = f32[4,64,128]{2,1,0:T(8,128)} custom-call(s32[1]{0:T(128)S(6)} %copy.10.refs_0_, f32[2]{0:T(128)} %refs_1_.1, s32[2,128]{1,0:T(2,128)} %bitcast.4, s32[1,128]{1,0:T(1,128)} %bitcast.5, f32[3,128,128]{2,1,0:T(8,128)} %bitcast.3, f32[128,4,128]{2,1,0:T(4,128)} %refs_5_.1, f32[128,256]{1,0:T(8,128)} %constant.4.clone.refs_6_, ...), custom_call_target="tpu_custom_call" | custom-call | tf_op jit(solution)/shard_map/grid_blocks/pallas_call | solution.py:311
  45.2 1.6 %copy.11 = f32[4,64,128]{2,1,0:T(8,128)} copy(f32[4,64,128]{2,1,0:T(8,128)} %grid_blocks.1) | data formatting | bytes 262144

commit v5 on v4

--- a/solution.py
+++ b/solution.py
@@ -21,8 +21,8 @@
 highest = lax.Precision.HIGHEST
 
 NEAREST = 12582912.0
-SIN = (6.283184916495431, -41.34158923268848, 81.59994332978006, -76.61447253122435, 41.34288235446963, -12.471243534886277)
-COS = (0.9999992107823215, -19.73898035576396, 64.92865742103214, -85.2716215342875, 58.7904921200778, -21.07110562755528)
+SIN = (4.442882919124344, -7.308245686508998, 3.606354218431858, -0.8461116503680876, 0.10982451641509068)
+COS = (1.4142134962552282, -6.978850948563766, 5.73946037690631, -1.8835579059813616, 0.31068802751622054)
 
 
 def horner(coefficients, z):
@@ -35,7 +35,8 @@
 def sincos_turns(turns):
     rest = turns - ((turns + NEAREST) - NEAREST)
     z = rest * rest
-    return rest * horner(SIN, z), horner(COS, z)
+    half = rest * horner(SIN, z)
+    return half * horner(COS, z), 1.0 - half * half
 
 
 def split(value):
@@ -190,16 +191,16 @@
     low_half = lax.broadcasted_iota(jnp.int32, (FOLD, width), 1) < 2 * SUB
 
     def picture(channel, block):
-        first, second, third = [coords_ref[axis, pl.ds(block, 1), :] for axis in range(3)]
+        factor = scale_ref[channel]
+        first, second, third = [coords_ref[axis, pl.ds(block, 1), :] * factor for axis in range(3)]
         waves = waves_ref[block]
-        factor = scale_ref[channel]
         depth = third * square
-        sine, cosine = sincos_turns((first * offset + depth) * factor)
+        sine, cosine = sincos_turns(first * offset + depth)
         real, imag = waves[2 * channel:2 * channel + 1, :], waves[2 * channel + 1:2 * channel + 2, :]
         left_high, left_low = split(
             jnp.concatenate([real * cosine - imag * sine, real * sine + imag * cosine], axis=1)
         )
-        sine, cosine = sincos_turns((second * offset + depth) * factor)
+        sine, cosine = sincos_turns(second * offset + depth)
         sine_high, sine_low = split(sine)
         cosine_high, cosine_low = split(cosine)
         right = jnp.concatenate(
@@ -213,8 +214,8 @@
         )
         product = dot_nt(jnp.concatenate([left_high, left_low], axis=0), right)
         product = product[:SUB] + product[SUB:]
-        product = product + pltpu.roll(product, 2 * SUB, 1)
-        return jnp.where(low_half, product[:FOLD], product[FOLD:])
+        upper, lower = product[:FOLD], product[FOLD:]
+        return jnp.where(low_half, upper, lower) + pltpu.roll(jnp.where(low_half, lower, upper), 2 * SUB, 1)
 
     def fill(channel, begin, end):
         def body(step, carry):
@@ -231,15 +232,15 @@
         named = lax.broadcasted_iota(jnp.int32, (subgrids, blocks), 0) == labels_ref[...]
         alive = lax.broadcasted_iota(jnp.int32, (subgrids, blocks), 1) < live_ref[0]
         choose = jnp.where(named & alive, 1.0, 0.0).astype(jnp.bfloat16)
-        for x in range(FOLD):
-            high, low = split(pictures_ref[x * blocks:(x + 1) * blocks])
-            both = jnp.dot(choose, jnp.concatenate([high, low], axis=1), preferred_element_type=jnp.float32)
-            both = both[:, :width] + both[:, width:]
-            for w in range(workers):
-                data_ref[channel, w // 2, w % 2, 0, x] = both[w * SUBW:(w + 1) * SUBW]
-
-    def begin(channel):
         for half in range(2):
+            for x in range(half * HALF, (half + 1) * HALF):
+                high, low = split(pictures_ref[x * blocks:(x + 1) * blocks])
+                both = jnp.dot(choose, jnp.concatenate([high, low], axis=1), preferred_element_type=jnp.float32)
+                both = both[:, :width] + both[:, width:]
+                for w in range(workers):
+                    data_ref[channel, w // 2, w % 2, 0, x] = both[w * SUBW:(w + 1) * SUBW]
+            if channel == 0 and half == 0:
+                pl.semaphore_wait(barrier, bits + tiles - 1)
             copies[channel, half] = step_copy(channel, half, 0)
             copies[channel, half].start()
 
@@ -263,8 +264,6 @@
 
     fill(0, 0, steps)
     merge(0)
-    pl.semaphore_wait(barrier, bits + tiles - 1)
-    begin(0)
     done = 0
     for step in range(bits):
         until = steps - (4 * steps // 5 >> step)
@@ -275,7 +274,6 @@
     spread_tiles(0)
     fill(1, done, steps)
     merge(1)
-    begin(1)
     for step in range(bits):
         advance(1, step)
     transform(1)

time: 46.9 us -> 47 us (level)
  no operation moved by 1% of the time
where the time goes in v5:
time: 47 us; the launch traced here: 46.8 us
  Pallas kernels  44.6 us (95%)
  local copies, waits for them, and re-layouts  1.57 us (3%)
  between operations  0.66 us (1%)
    pallas_call x1, Pallas kernels, gridded(): pl.pallas_call(functools.partial(grid_kernel, workers, tiles), out_shape=...  44.6 us
    unnamed x1, local copies, waits for them, and re-layouts  1.57 us

profile of v5, /device:TPU:0, one launch (start us, length us, event | category | flops | bytes accessed | tf_op | source)
XLA Modules:
  0.0 46.8 jit_solution(16960885865007161242)
XLA Ops:
  0.7 44.6 %grid_blocks.1 = f32[4,64,128]{2,1,0:T(8,128)} custom-call(s32[1]{0:T(128)S(6)} %copy.10.refs_0_, f32[2]{0:T(128)} %refs_1_.1, s32[2,128]{1,0:T(2,128)} %bitcast.4, s32[1,128]{1,0:T(1,128)} %bitcast.5, f32[3,128,128]{2,1,0:T(8,128)} %bitcast.3, f32[128,4,128]{2,1,0:T(4,128)} %refs_5_.1, f32[128,256]{1,0:T(8,128)} %constant.4.clone.refs_6_, ...), custom_call_target="tpu_custom_call" | custom-call | tf_op jit(solution)/shard_map/grid_blocks/pallas_call | solution.py:309
  45.3 1.6 %copy.11 = f32[4,64,128]{2,1,0:T(8,128)} copy(f32[4,64,128]{2,1,0:T(8,128)} %grid_blocks.1) | data formatting | bytes 262144

commit v6 on v5

--- a/solution.py
+++ b/solution.py
@@ -16,7 +16,7 @@
 SUBW = 16
 FOLD = SUB // 2
 HALF = FOLD // 2
-UNROLL = 16
+UNROLL = 32
 MESH = pl.DeviceIdType.MESH
 highest = lax.Precision.HIGHEST
 

time: 47 us -> 45.4 us (0.966)
  Pallas kernels: 44.6 us -> 43 us
    pallas_call x1, Pallas kernels: 44.6 us -> 43 us  [gridded(): pl.pallas_call(functools.partial(grid_kernel, workers, tiles), out_shape=...]
where the time goes in v6:
time: 45.4 us; the launch traced here: 45.3 us
  Pallas kernels  43 us (95%)
  local copies, waits for them, and re-layouts  1.57 us (3%)
  between operations  0.66 us (1%)
    pallas_call x1, Pallas kernels, gridded(): pl.pallas_call(functools.partial(grid_kernel, workers, tiles), out_shape=...  43 us
    unnamed x1, local copies, waits for them, and re-layouts  1.57 us

profile of v6, /device:TPU:0, one launch (start us, length us, event | category | flops | bytes accessed | tf_op | source)
XLA Modules:
  0.0 45.3 jit_solution(10454652475711665706)
XLA Ops:
  0.7 43.0 %grid_blocks.1 = f32[4,64,128]{2,1,0:T(8,128)} custom-call(s32[1]{0:T(128)S(6)} %copy.10.refs_0_, f32[2]{0:T(128)} %refs_1_.1, s32[2,128]{1,0:T(2,128)} %bitcast.4, s32[1,128]{1,0:T(1,128)} %bitcast.5, f32[3,128,128]{2,1,0:T(8,128)} %bitcast.3, f32[128,4,128]{2,1,0:T(4,128)} %refs_5_.1, f32[128,256]{1,0:T(8,128)} %constant.4.clone.refs_6_, ...), custom_call_target="tpu_custom_call" | custom-call | tf_op jit(solution)/shard_map/grid_blocks/pallas_call | solution.py:309
  43.7 1.6 %copy.11 = f32[4,64,128]{2,1,0:T(8,128)} copy(f32[4,64,128]{2,1,0:T(8,128)} %grid_blocks.1) | data formatting | bytes 262144
